TPU v7x, 32 devices: a whole 2x2x4 slice. The times are simulated.
32 devices in a mesh: table: 2 (over x), image: 16 (over z, y, core).
Axes of the slice: x: 2, y: 2, z: 4, core: 2. Of those that a mesh axis runs over, the one named last changes fastest.
Arguments:
- traces: bfloat16 [512, 1920], P(('table', 'image')), may hold values from -6 to 6
- aperture: int32 [512, 4], P(('table', 'image')), may hold values from 0 to 15, all different within a row; in each aligned block of 16 rows (0 to 15, 16 to 31, ...) at most 8 rows name the same one
- bucket: int32 [512], P(('table', 'image')), may hold values from 0 to 3
- table_node: int32 [512, 4], P(('table', 'image')), may hold values from 0 to 15
- entry_gain: bfloat16 [512, 4], P(('table', 'image')), may hold values from 0.5 to 2
- travel: float32 [16, 16, 1024], P('image', None, 'table'), may hold values from 1 to 1918
- spread: float32 [16, 16, 1024], P('image', None, 'table'), may hold values from 0.1 to 1
Outputs:
- image: float32 [16, 1024], P('image', 'table')
Inputs may be any that keep to these rules, and one draw needn't show every extreme that they name: `aperture`: each trace names 4 different tiles. Among the 16 traces of one device at most 8 name the same tile, and in every draw some tile is named by exactly 8 of them.
All inputs are finite; a program needn't handle non-finite values.
Results may differ from a plain program's by a relative error of at most 0.0024.
Values may be sent and summed in bfloat16 or wider, within the bound.
A program may use at most 128 MiB of HBM per device.

v0:
```python
import math

import jax
import jax.numpy as jnp
from jax import lax
from jax.sharding import PartitionSpec as P

max_lag = 7


def antialias(trace_rows, filter_index):
    half_width = (2 + 2 * filter_index).astype(jnp.float32)[..., None]
    length = trace_rows.shape[-1]
    widths = [(0, 0)] * (trace_rows.ndim - 1) + [(max_lag, max_lag)]
    padded = jnp.pad(trace_rows, widths)
    summed = jnp.zeros(trace_rows.shape, jnp.float32)
    for sample_lag in range(-max_lag, max_lag + 1):
        ramp_weight = jnp.maximum(half_width - abs(sample_lag), 0.0) / (half_width * half_width)
        window = lax.slice_in_dim(
            padded, max_lag + sample_lag, max_lag + sample_lag + length, axis=trace_rows.ndim - 1
        )
        summed = summed + ramp_weight * window
    return summed


def interpolate(stack_tile, travel_tile, spread_tile):
    floor_value = jnp.floor(travel_tile)
    fraction = travel_tile - floor_value
    lower_index = floor_value.astype(jnp.int32)
    shifted = jnp.pad(stack_tile[:, 1:], ((0, 0), (0, 1)))
    paired = jnp.stack([stack_tile, shifted], axis=-1)
    picked = jnp.take_along_axis(paired, lower_index[:, :, None], axis=1)
    lower_value = picked[:, :, 0]
    upper_value = picked[:, :, 1]
    return jnp.sum(spread_tile * ((1.0 - fraction) * lower_value + fraction * upper_value), axis=0)


def per_device(traces, aperture, bucket, table_node, entry_gain, travel, spread):
    tiles = lax.axis_size("image")
    groups = lax.axis_size("table")
    trace_count, samples = traces.shape
    aper_count = aperture.shape[1]
    node_count = travel.shape[1]
    capacity = max(2, 2 * trace_count * aper_count // tiles)
    entries = trace_count * aper_count
    destination = aperture.reshape(entries)
    member = (destination[:, None] == jnp.arange(tiles, dtype=jnp.int32)[None, :]).astype(jnp.int32)
    earlier = jnp.cumsum(member, axis=0) - member
    slot_index = jnp.sum(earlier * member, axis=1)
    source_row = jnp.arange(entries, dtype=jnp.int32) // aper_count
    flat_nodes = table_node.reshape(entries)
    flat_gains = entry_gain.reshape(entries)
    node_slots = jnp.zeros((capacity, tiles), jnp.int32).at[slot_index, destination].set(flat_nodes)
    raw_slots = (
        jnp.zeros((capacity, tiles, samples), jnp.bfloat16)
        .at[slot_index, destination]
        .set(traces[source_row])
    )
    gain_slots = (
        jnp.zeros((capacity, tiles), jnp.bfloat16).at[slot_index, destination].set(flat_gains)
    )
    filter_slots = (
        jnp.zeros((capacity, tiles), jnp.int32).at[slot_index, destination].set(bucket[source_row])
    )
    raw_part = lax.all_to_all(raw_slots, "image", split_axis=1, concat_axis=1, tiled=True)
    gain_part = lax.all_to_all(gain_slots, "image", split_axis=1, concat_axis=1, tiled=True)
    filter_part = lax.all_to_all(filter_slots, "image", split_axis=1, concat_axis=1, tiled=True)
    node_part = lax.all_to_all(node_slots, "image", split_axis=1, concat_axis=1, tiled=True)
    filtered = antialias(raw_part.astype(jnp.float32), filter_part)
    weighted = (gain_part.astype(jnp.float32)[..., None] * filtered).astype(jnp.bfloat16)
    slot_total = tiles * capacity
    flat_values = weighted.reshape(slot_total, samples)
    node_member = (
        node_part.reshape(slot_total)[:, None] == jnp.arange(node_count, dtype=jnp.int32)[None, :]
    ).astype(jnp.bfloat16)
    stack = lax.dot_general(
        node_member, flat_values, (((0,), (0,)), ((), ())), preferred_element_type=jnp.float32
    )
    scale = 1.0 / math.sqrt(trace_count * groups * aper_count)
    summed_stack = lax.psum(stack, "table")
    return (interpolate(summed_stack, travel[0], spread[0]) * scale)[None, :]


def solution(mesh):
    in_specs = (
        P(("table", "image"), None),
        P(("table", "image"), None),
        P(("table", "image")),
        P(("table", "image"), None),
        P(("table", "image"), None),
        P("image", None, "table"),
        P("image", None, "table"),
    )
    out_specs = P("image", "table")
    return jax.shard_map(
        per_device, mesh=mesh, in_specs=in_specs, out_specs=out_specs, check_vma=False
    )
```

profile of v0, /device:TPU:0, one launch (start us, length us, event | category | flops | bytes accessed | tf_op | source)
XLA Modules:
  0.0 235.1 jit_solution(4942274203572084065)
XLA Ops:
  6.5 0.0 copy-start
  6.5 0.8 copy.41
  7.3 0.1 eq.30
  7.4 0.1 reshape.171
  7.5 0.1 fusion.22
  7.6 0.1 reduce_window_sum.11
  7.7 0.2 select_reduce_fusion
  7.8 0.8 copy.46
  8.6 0.1 reshape.206
  8.7 3.5 %scatter_fusion.1 = bf16[8,16]{1,0:T(8,128)(2,1)S(1)} fusion(bf16[8,16]{1,0:T(8,128)(2,1)S(1)} %broadcast_in_dim.11, s32[64]{0:T(128)S(1)} %fusion.25, bf16[64]{0:T(256)(128)(2,1)S(1)} %reshape.206), kind=kCustom, calls=%fused_computation.4 | custom fusion | bytes 896 | tf_op jit(solution)/shard_map/scatter | solution.py:60
  12.3 0.7 copy.47
  12.9 7.4 %all-to-all-start.1 = ((bf16[8,16,1]{0,2,1:T(2,128)(2,1)}), bf16[8,16,1]{0,2,1:T(2,128)(2,1)S(1)}, u32[]{:S(2)}, u32[]{:S(2)}) async-start(bf16[8,16,1]{0,2,1:T(2,128)(2,1)} %copy.47), calls=%async_computation.1 | async-start | bytes 16384 | tf_op jit(solution)/shard_map/all_to_all | solution.py:66
  20.4 1.4 gather_fusion
  21.8 3.5 %scatter_fusion.2 = s32[8,16]{1,0:T(8,128)S(1)} fusion(s32[8,16]{1,0:T(8,128)S(1)} %broadcast.222.clone, s32[64]{0:T(128)S(1)} %fusion.25, s32[64]{0:T(128)S(1)} %gather_fusion), kind=kCustom, calls=%fused_computation.5 | custom fusion | bytes 1280 | tf_op jit(solution)/shard_map/scatter | solution.py:63
  25.3 0.7 copy.49
  25.9 0.8 all-to-all-done.1
  26.7 5.2 %all-to-all-start.2 = ((s32[8,16,1]{0,2,1:T(1,128)}), s32[8,16,1]{0,2,1:T(1,128)S(1)}, u32[]{:S(2)}, u32[]{:S(2)}) async-start(s32[8,16,1]{0,2,1:T(1,128)} %copy.49), calls=%async_computation.2 | async-start | bytes 16384 | tf_op jit(solution)/shard_map/all_to_all | solution.py:67
  31.9 0.8 copy.43
  32.7 0.1 reshape.200
  32.8 3.5 %scatter_fusion = s32[8,16]{1,0:T(8,128)S(1)} fusion(s32[8,16]{1,0:T(8,128)S(1)} %broadcast.222.clone.1, s32[64]{0:T(128)S(1)} %fusion.25, s32[64]{0:T(128)S(1)} %reshape.200), kind=kCustom, calls=%fused_computation.3 | custom fusion | bytes 1280 | tf_op jit(solution)/shard_map/scatter | solution.py:53
  36.3 0.7 copy.44
  36.9 1.4 all-to-all-done.2
  38.4 4.6 %all-to-all-start = ((s32[8,16,1]{0,2,1:T(1,128)}), s32[8,16,1]{0,2,1:T(1,128)S(1)}, u32[]{:S(2)}, u32[]{:S(2)}) async-start(s32[8,16,1]{0,2,1:T(1,128)} %copy.44), calls=%async_computation | async-start | bytes 16384 | tf_op jit(solution)/shard_map/all_to_all | solution.py:68
  43.0 0.0 copy-done
  43.0 0.0 copy-start.1
  43.0 0.8 gather_fusion.1
  43.8 6.3 %scatter_fusion.3 = bf16[8,16,1920]{2,1,0:T(8,128)(2,1)S(1)} fusion(bf16[8,16,1920]{2,1,0:T(8,128)(2,1)S(1)} %broadcast_in_dim.12, s32[64]{0:T(128)S(1)} %fusion.25, bf16[64,1920]{1,0:T(8,128)(2,1)S(1)} %gather_fusion.1), kind=kCustom, calls=%fused_computation.6 | custom fusion | bytes 737792 | tf_op jit(solution)/shard_map/scatter | solution.py:57
  50.1 0.9 copy.51
  50.9 0.0 all-to-all-done
  50.9 6.0 %all-to-all-start.3 = ((bf16[8,16,1920]{2,0,1:T(8,128)(2,1)}), bf16[8,16,1920]{2,0,1:T(8,128)(2,1)S(1)}, u32[]{:S(2)}, u32[]{:S(2)}) async-start(bf16[8,16,1920]{2,0,1:T(8,128)(2,1)} %copy.51), calls=%async_computation.3 | async-start | bytes 983040 | tf_op jit(solution)/shard_map/all_to_all | solution.py:65
  56.9 0.0 all-reduce.4.cloned.1.call-start
  57.0 0.0 copy-done.1
  57.0 0.1 copy.48
  57.1 0.1 copy.45
  57.2 0.1 eq.34
  57.3 0.1 copy.50
  57.4 13.3 %all-to-all-done.3 = bf16[8,16,1920]{2,0,1:T(8,128)(2,1)S(1)} async-done(((bf16[8,16,1920]{2,0,1:T(8,128)(2,1)}), bf16[8,16,1920]{2,0,1:T(8,128)(2,1)S(1)}, u32[]{:S(2)}, u32[]{:S(2)}) %all-to-all-start.3) | async-done | bytes 491552 | tf_op jit(solution)/shard_map/all_to_all | solution.py:65
  70.7 0.1 copy_convert_fusion
  70.8 4.0 %multiply_convert_fusion = bf16[8,16,1920]{2,1,0:T(8,128)(2,1)S(1)} fusion(f32[8,16,1920]{2,1,0:T(8,128)S(1)} %copy_convert_fusion, f32[8,16]{1,0:T(8,128)S(1)} %get-tuple-element.6, f32[8,16]{1,0:T(8,128)S(1)} %get-tuple-element.7, f32[8,16]{1,0:T(8,128)S(1)} %get-tuple-element.8, f32[8,16]{1,0:T(8,128)S(1)} %get-tuple-element.9, ...), kind=kLoop, calls=%fused_computation.7 | loop fusion | flops 7618560 | bytes 1479168 | tf_op jit(solution)/shard_map/convert_element_type | solution.py:70
  74.8 0.9 fusion.11
  75.7 0.0 all-reduce.4.cloned.1.call-update
  75.8 20.8 %all-reduce.4.cloned.1.call-done = f32[16,1920]{1,0:T(8,128)} async-done(((f32[16,1920]{1,0:T(8,128)}), f32[16,1920]{1,0:T(8,128)}) %all-reduce.4.cloned.1.call-update) | async-done | bytes 122896 | tf_op jit(solution)/shard_map/psum | solution.py:80
  96.6 1.0 slice.83
  97.6 0.9 pad_maximum_fusion
  98.5 7.8 %copy.53 = f32[16,1920,2]{2,1,0:T(8,128)} copy(f32[16,1920,2]{1,0,2:T(8,128)S(1)} %pad_maximum_fusion) | data formatting | bytes 491520 | tf_op jit(solution)/shard_map/stack | solution.py:31
  106.3 118.4 %gather_fusion.2 = f32[8192,2]{1,0:T(8,128)} fusion(f32[16,1920,2]{2,1,0:T(8,128)} %copy.53, s32[8192]{0:T(1024)S(1)} %bitcast.70), kind=kCustom, calls=%fused_computation.2 | custom fusion | bytes 196608 | tf_op jit(solution)/shard_map/jit(take_along_axis)/gather | solution.py:32
  224.8 2.8 %copy.54 = f32[16,512,2]{1,0,2:T(8,128)S(1)} copy(f32[16,512,2]{2,1,0:T(8,128)} %bitcast.74) | data formatting | bytes 131072 | tf_op jit(solution)/shard_map/jit(take_along_axis)/gather | solution.py:32
  227.7 0.6 broadcast_multiply_fusion
  (17 shorter events, 0.2 us)
Async XLA Ops:
  6.5 36.4 %copy-start = (bf16[16,1920]{1,0:T(8,128)(2,1)S(1)}, bf16[16,1920]{1,0:T(8,128)(2,1)}, u32[]{:S(2)}) copy-start(bf16[16,1920]{1,0:T(8,128)(2,1)} %param.7) | copy-start | bytes 184324
  12.9 13.8 %all-to-all-start.1 = ((bf16[8,16,1]{0,2,1:T(2,128)(2,1)}), bf16[8,16,1]{0,2,1:T(2,128)(2,1)S(1)}, u32[]{:S(2)}, u32[]{:S(2)}) async-start(bf16[8,16,1]{0,2,1:T(2,128)(2,1)} %copy.47), calls=%async_computation.1 | async-start | bytes 16384 | tf_op jit(solution)/shard_map/all_to_all | solution.py:66
  26.7 11.6 %all-to-all-start.2 = ((s32[8,16,1]{0,2,1:T(1,128)}), s32[8,16,1]{0,2,1:T(1,128)S(1)}, u32[]{:S(2)}, u32[]{:S(2)}) async-start(s32[8,16,1]{0,2,1:T(1,128)} %copy.49), calls=%async_computation.2 | async-start | bytes 16384 | tf_op jit(solution)/shard_map/all_to_all | solution.py:67
  38.4 12.6 %all-to-all-start = ((s32[8,16,1]{0,2,1:T(1,128)}), s32[8,16,1]{0,2,1:T(1,128)S(1)}, u32[]{:S(2)}, u32[]{:S(2)}) async-start(s32[8,16,1]{0,2,1:T(1,128)} %copy.44), calls=%async_computation | async-start | bytes 16384 | tf_op jit(solution)/shard_map/all_to_all | solution.py:68
  43.0 14.0 %copy-start.1 = (f32[1,16,512]{2,1,0:T(8,128)S(1)}, f32[1,16,512]{2,1,0:T(8,128)}, u32[]{:S(2)}) copy-start(f32[1,16,512]{2,1,0:T(8,128)} %param.12) | copy-start | bytes 98308
  50.9 19.8 %all-to-all-start.3 = ((bf16[8,16,1920]{2,0,1:T(8,128)(2,1)}), bf16[8,16,1920]{2,0,1:T(8,128)(2,1)S(1)}, u32[]{:S(2)}, u32[]{:S(2)}) async-start(bf16[8,16,1920]{2,0,1:T(8,128)(2,1)} %copy.51), calls=%async_computation.3 | async-start | bytes 983040 | tf_op jit(solution)/shard_map/all_to_all | solution.py:65
  56.9 39.7 %all-reduce.4.cloned.1.call-start = ((), (), s32[]{:S(2)}) async-start(), calls=%async_computation.4 | async-start | bytes 245760 | tf_op jit(solution)/shard_map/psum | solution.py:80
  224.8 2.9 %copy-start.2 = (f32[1,16,512]{2,1,0:T(8,128)S(1)}, f32[1,16,512]{2,1,0:T(8,128)}, u32[]{:S(2)}) copy-start(f32[1,16,512]{2,1,0:T(8,128)} %param.13) | copy-start | bytes 98308
Sparse Core Ops, SparseCore 0:
  75.9 20.6 all-reduce.3
where the time goes:
time: 236 us; the launch traced here: 235 us
  local copies, waits for them, and re-layouts  155 us (66%)
  waiting for transfers between devices  36.4 us (15%)
  starting transfers between devices  23.2 us (10%)
  between operations  13.6 us (6%)
  other arithmetic  6.02 us (3%)
    gather x2, local copies, waits for them, and re-layouts, interpolate(): picked = jnp.take_along_axis(paired, lower_index[:, :, None], axis=1)  121 us
    psum x1, waiting for transfers between devices, per_device(): summed_stack = lax.psum(stack, 'table')  20.8 us
    all_to_all x1, waiting for transfers between devices, per_device(): lax.all_to_all(raw_slots, 'image', split_axis=1, concat_axis=1, tiled=True)  13.3 us
    another operation x2, local copies, waits for them, and re-layouts, interpolate(): paired = jnp.stack([stack_tile, shifted], axis=-1)  7.79 us
    all_to_all x1, starting transfers between devices, per_device(): lax.all_to_all(gain_slots, 'image', split_axis=1, concat_axis=1, tiled=True)  7.39 us
    scatter x2, local copies, waits for them, and re-layouts, per_device(): raw_slots = jnp.zeros((capacity, tiles, samples), jnp.bfloat16).at[slot_i...  7.15 us
    scatter x2, local copies, waits for them, and re-layouts, per_device(): jnp.zeros((capacity, tiles), jnp.int32).at[slot_index, destination]  6.91 us
    all_to_all x1, starting transfers between devices, per_device(): lax.all_to_all(raw_slots, 'image', split_axis=1, concat_axis=1, tiled=True)  6 us
  transfers between devices with their start and end apart: 5, of which 4 were waited for; matrix products, arithmetic and copies ran while one was open for 8% of the time, Pallas kernels for 0%

commit v1 on v0

v1 whole, which is shorter than its diff:
```python
import functools
import math

import jax
import jax.numpy as jnp
from jax import lax
from jax.experimental import pallas as pl
from jax.experimental.pallas import tpu as pltpu
from jax.sharding import PartitionSpec as P

LANES = 128
FILTERS = 4
MAX_LAG = 7
MESH = pl.DeviceIdType.MESH


def split_axis(count):
    if count == 16:
        return (4, 2, 2)
    root = math.isqrt(count)
    if root * root == count:
        return (root, root, 1)
    return (count, 1, 1)


def both(first, second):
    if first is None:
        return second
    if second is None:
        return first
    return jnp.logical_and(first, second)


def guarded(cond, action):
    if cond is None:
        action()
    else:
        pl.when(cond)(action)


def neighbours(size, at):
    if size == 1:
        return []
    if size == 2:
        return [(1, 1 - at, None)]
    return [(1, at + 1, at < size - 1), (-1, at - 1, at > 0)]


def arrivals(size, at):
    if size == 1:
        return []
    if size == 2:
        return [(1, 1 - at, None, 1, None, None)]
    found = []
    for distance in range(1, size):
        for step in (1, -1):
            source = at - step * distance
            valid = source >= 0 if step > 0 else source < size
            onward = at < size - 1 if step > 0 else at > 0
            found.append((distance, source, valid, step, at + step, onward))
    return found


def eye_column(row, count):
    across = lax.broadcasted_iota(jnp.int32, (count, count), 1)
    down = lax.broadcasted_iota(jnp.int32, (count, count), 0)
    return jnp.sum(jnp.where(across == down, row, 0.0), axis=1, keepdims=True)


def selection(aperture, bucket, node, gain, nodes, half):
    count = aperture.shape[1]
    lane = lax.broadcasted_iota(jnp.int32, (count, 2 * half), 1)
    low = lane < half
    tile = jnp.where(low, lane, lane - half).astype(jnp.float32)
    offset = eye_column(bucket.astype(jnp.float32) * nodes, count)
    total = jnp.zeros((count, 2 * half), jnp.float32)
    for a in range(aperture.shape[0]):
        named = eye_column(aperture[a : a + 1].astype(jnp.float32), count)
        row = eye_column(node[a : a + 1].astype(jnp.float32), count) + offset
        weight = eye_column(gain[a : a + 1].astype(jnp.float32), count)
        total = total + jnp.where(named == tile, jnp.where(low, weight, row), 0.0)
    return total


def triangle(bucket, lag):
    half = 2 + 2 * bucket
    return max(half - lag, 0) / (half * half)


def partial_image(stack, upper, travel, spread):
    floor_value = jnp.floor(travel)
    fraction = travel - floor_value
    lower = floor_value.astype(jnp.int32)
    chunk = lax.shift_right_logical(lower, 7)
    inner = jnp.bitwise_and(lower, LANES - 1)
    pieces = []
    for c in range(travel.shape[1] // LANES):
        cells = slice(c * LANES, (c + 1) * LANES)
        here, within = chunk[:, cells], inner[:, cells]
        low = jnp.zeros(here.shape, jnp.float32)
        high = jnp.zeros(here.shape, jnp.float32)
        for k in range(stack.shape[1] // LANES):
            samples = slice(k * LANES, (k + 1) * LANES)
            mine = here == k
            picked = jnp.take_along_axis(stack[:, samples], within, axis=1, mode="promise_in_bounds")
            above = jnp.take_along_axis(upper[:, samples], within, axis=1, mode="promise_in_bounds")
            low = jnp.where(mine, picked, low)
            high = jnp.where(mine, above, high)
        part = fraction[:, cells]
        value = spread[:, cells] * ((1.0 - part) * low + part * high)
        pieces.append(jnp.sum(value, axis=0, keepdims=True))
    return jnp.concatenate(pieces, axis=1)


def kernel(
    sizes, groups, half, scale,
    aperture_ref, bucket_ref, node_ref, gain_ref, traces_ref, travel_ref, spread_ref,
    out_ref,
    blocks, travels, spreads, parts, outgoing,
    send_sem, recv_sem, table_send, table_recv, part_send, part_recv,
):
    size_z, size_y, size_c = sizes
    me = lax.axis_index("image")
    group = lax.axis_index("table")
    z = me // (size_y * size_c)
    y = lax.rem(me // size_c, size_y)
    core = lax.rem(me, size_c)
    count, samples = traces_ref.shape
    nodes = travel_ref.shape[0]
    cells = travel_ref.shape[1]

    def index(at_z, at_y, at_c):
        return (at_z * size_y + at_y) * size_c + at_c

    links_z, links_y, links_c = neighbours(size_z, z), neighbours(size_y, y), neighbours(size_c, core)
    others = [lax.rem(group + r, groups) for r in range(1, groups)]

    barrier = pltpu.get_barrier_semaphore()
    partners = [(index(to, y, core), cond) for _, to, cond in links_z]
    partners += [(index(z, to, core), cond) for _, to, cond in links_y]
    partners += [(index(z, y, to), cond) for _, to, cond in links_c]
    for to, cond in partners:
        guarded(cond, lambda to=to: pl.semaphore_signal(barrier, inc=1, device_id=(group, to), device_id_type=MESH))
    for other in others:
        pl.semaphore_signal(barrier, inc=1, device_id=(other, me), device_id_type=MESH)

    blocks[me, :, :samples] = traces_ref[...]
    blocks[me, :, samples:] = selection(
        aperture_ref[...], bucket_ref[...], node_ref[...], gain_ref[...], nodes, half
    ).astype(jnp.bfloat16)

    expected = len(others) + sum(1 if cond is None else cond.astype(jnp.int32) for _, cond in partners)
    pl.semaphore_wait(barrier, expected)

    started = []

    def send(slot, direction, to, cond, under=None):
        copy = pltpu.make_async_remote_copy(
            src_ref=blocks.at[slot],
            dst_ref=blocks.at[slot],
            send_sem=send_sem.at[direction, slot],
            recv_sem=recv_sem.at[slot],
            device_id=(group, to),
            device_id_type=MESH,
        )
        guarded(cond, copy.start)
        started.append((slot, direction, under, cond))

    def receive(slot):
        pltpu.make_async_remote_copy(
            src_ref=blocks.at[slot],
            dst_ref=blocks.at[slot],
            send_sem=send_sem.at[0, slot],
            recv_sem=recv_sem.at[slot],
            device_id=(group, me),
            device_id_type=MESH,
        ).wait_recv()

    def number(base, step):
        return base if step > 0 else base + 1

    def send_y(slot, under):
        for step, to, cond in links_y:
            send(slot, number(2, step), index(z, to, core), cond, under)

    def send_c(slot, under):
        for step, to, cond in links_c:
            send(slot, number(4, step), index(z, y, to), cond, under)

    for step, to, cond in links_z:
        send(me, number(0, step), index(to, y, core), cond)
    send_y(me, None)
    send_c(me, None)
    table_copies = []
    for r, other in enumerate(others):
        for which, (source, landing) in enumerate(((travel_ref, travels), (spread_ref, spreads))):
            copy = pltpu.make_async_remote_copy(
                src_ref=source,
                dst_ref=landing.at[group],
                send_sem=table_send.at[which, r],
                recv_sem=table_recv.at[which, group],
                device_id=(other, me),
                device_id_type=MESH,
            )
            copy.start()
            table_copies.append(copy)

    events = []
    along_z = [(0, z, None)]
    for distance, source, valid, step, onward, can in arrivals(size_z, z):
        along_z.append((distance, source, valid))

        def came_z(slot=index(source, y, core), valid=valid, step=step, onward=onward, can=can):
            def run():
                receive(slot)
                send(slot, number(0, step), index(onward, y, core), can, valid)
                send_y(slot, valid)
                send_c(slot, valid)

            guarded(valid, run)

        events.append((distance, 0, came_z))
    for far, source_z, valid_z in along_z:
        for distance, source, valid, step, onward, can in arrivals(size_y, y):

            def came_y(
                slot=index(source_z, source, core),
                valid=both(valid_z, valid), step=step, onward=onward, can=can,
            ):
                def run():
                    receive(slot)
                    if onward is not None:
                        send(slot, number(2, step), index(z, onward, core), can, valid)
                    send_c(slot, valid)

                guarded(valid, run)

            events.append((far + distance, 1, came_y))
    for _, _, run in sorted(events, key=lambda e: e[:2]):
        run()
    for _, source, valid, _, _, _ in arrivals(size_c, core):
        for at_z in range(size_z):
            for at_y in range(size_y):
                receive(index(at_z, at_y, source))

    total = size_z * size_y * size_c * count
    chosen = blocks[:, :, samples:].reshape(total, 2 * half).astype(jnp.float32)
    lane = lax.broadcasted_iota(jnp.int32, (1, 2 * half), 1)
    weight = jnp.sum(jnp.where(lane == me, chosen, 0.0), axis=1, keepdims=True)
    row = jnp.sum(jnp.where(lane == me + half, chosen, 0.0), axis=1, keepdims=True)
    rows = lax.broadcasted_iota(jnp.int32, (1, FILTERS * nodes), 1).astype(jnp.float32)
    member = jnp.where(row == rows, weight, 0.0).astype(jnp.bfloat16)
    stacked = lax.dot_general(
        member,
        blocks[:, :, :samples].reshape(total, samples),
        (((0,), (0,)), ((), ())),
        preferred_element_type=jnp.float32,
    )
    width = samples + LANES
    stacked = jnp.concatenate([stacked, jnp.zeros((FILTERS * nodes, LANES), jnp.float32)], axis=1)
    by_bucket = [stacked[b * nodes : (b + 1) * nodes] for b in range(FILTERS)]
    stack = None
    for lag in range(MAX_LAG + 1):
        mixed = None
        for b in range(FILTERS):
            if (level := triangle(b, lag)) > 0:
                term = by_bucket[b] * level
                mixed = term if mixed is None else mixed + term
        if lag == 0:
            stack = mixed
        else:
            stack = stack + (pltpu.roll(mixed, lag, 1) + pltpu.roll(mixed, width - lag, 1))
    upper = pltpu.roll(stack, width - 1, 1)[:, :samples]
    stack = stack[:, :samples]

    part_copies = []
    for r, other in enumerate(others):
        for which, landing in enumerate((travels, spreads)):
            pltpu.make_async_remote_copy(
                src_ref=landing.at[other],
                dst_ref=landing.at[other],
                send_sem=table_send.at[which, r],
                recv_sem=table_recv.at[which, other],
                device_id=(other, me),
                device_id_type=MESH,
            ).wait_recv()
        outgoing[r] = partial_image(stack, upper, travels[other], spreads[other])
        copy = pltpu.make_async_remote_copy(
            src_ref=outgoing.at[r],
            dst_ref=parts.at[group],
            send_sem=part_send.at[r],
            recv_sem=part_recv.at[group],
            device_id=(other, me),
            device_id_type=MESH,
        )
        copy.start()
        part_copies.append(copy)
    image = partial_image(stack, upper, travel_ref[...], spread_ref[...])
    for slot, direction, under, cond in started:
        copy = pltpu.make_async_remote_copy(
            src_ref=blocks.at[slot],
            dst_ref=blocks.at[slot],
            send_sem=send_sem.at[direction, slot],
            recv_sem=recv_sem.at[slot],
            device_id=(group, me),
            device_id_type=MESH,
        )
        guarded(both(under, cond), copy.wait_send)
    for copy in table_copies:
        copy.wait_send()
    for r, other in enumerate(others):
        pltpu.make_async_remote_copy(
            src_ref=outgoing.at[r],
            dst_ref=parts.at[other],
            send_sem=part_send.at[r],
            recv_sem=part_recv.at[other],
            device_id=(other, me),
            device_id_type=MESH,
        ).wait_recv()
        image = image + parts[other]
    for copy in part_copies:
        copy.wait_send()
    out_ref[...] = image * scale


def per_device(traces, aperture, bucket, table_node, entry_gain, travel, spread):
    tiles = lax.axis_size("image")
    groups = lax.axis_size("table")
    count, samples = traces.shape
    nodes, cells = travel.shape[1], travel.shape[2]
    half = -(-tiles // (LANES // 2)) * (LANES // 2)
    scale = 1.0 / math.sqrt(count * groups * aperture.shape[1])
    vmem = pl.BlockSpec(memory_space=pltpu.VMEM)
    return pl.pallas_call(
        functools.partial(kernel, split_axis(tiles), groups, half, scale),
        out_shape=jax.ShapeDtypeStruct((1, cells), jnp.float32),
        in_specs=[vmem] * 7,
        out_specs=vmem,
        scratch_shapes=[
            pltpu.VMEM((tiles, count, samples + 2 * half), jnp.bfloat16),
            pltpu.VMEM((groups, nodes, cells), jnp.float32),
            pltpu.VMEM((groups, nodes, cells), jnp.float32),
            pltpu.VMEM((groups, 1, cells), jnp.float32),
            pltpu.VMEM((max(groups - 1, 1), 1, cells), jnp.float32),
            pltpu.SemaphoreType.DMA((6, tiles)),
            pltpu.SemaphoreType.DMA((tiles,)),
            pltpu.SemaphoreType.DMA((2, max(groups - 1, 1))),
            pltpu.SemaphoreType.DMA((2, groups)),
            pltpu.SemaphoreType.DMA((max(groups - 1, 1),)),
            pltpu.SemaphoreType.DMA((groups,)),
        ],
        compiler_params=pltpu.CompilerParams(
            collective_id=0, has_side_effects=True, vmem_limit_bytes=48 * 1024 * 1024
        ),
        cost_estimate=pl.CostEstimate(flops=10**8, bytes_accessed=10**6, transcendentals=0),
    )(aperture.T, bucket.reshape(1, count), table_node.T, entry_gain.T, traces, travel[0], spread[0])


def solution(mesh):
    in_specs = (
        P(("table", "image"), None),
        P(("table", "image"), None),
        P(("table", "image")),
        P(("table", "image"), None),
        P(("table", "image"), None),
        P("image", None, "table"),
        P("image", None, "table"),
    )
    out_specs = P("image", "table")
    return jax.shard_map(
        per_device, mesh=mesh, in_specs=in_specs, out_specs=out_specs, check_vma=False
    )
```

time: 236 us -> 26.9 us (0.11)
  local copies, waits for them, and re-layouts: 155 us -> 3.63 us
  waiting for transfers between devices: 36.4 us -> 0 us
  starting transfers between devices: 23.2 us -> 0 us
  Pallas kernels: 0 us -> 22.9 us
  between operations: 13.6 us -> 0.02 us
  other arithmetic: 6.02 us -> 0 us
    gather x4 -> x0, local copies, waits for them, and re-layouts: 123 us -> none  [the longest x2 121 us: interpolate(): picked = jnp.take_along_axis(paired, lower_index[:, :, None], axis=1)]
    all_to_all x4 -> x0, starting transfers between devices: 23.2 us -> none  [the longest x1 7.39 us: per_device(): lax.all_to_all(gain_slots, 'image', split_axis=1, concat_axis=1, tiled=True)]
    pallas_call x0 -> x1, Pallas kernels: none -> 22.9 us  [per_device(): pl.pallas_call(functools.partial(kernel, split_axis(tiles), groups, half,...]
    psum x1 -> x0, waiting for transfers between devices: 20.8 us -> none  [per_device(): summed_stack = lax.psum(stack, 'table')]
    scatter x5 -> x0, local copies, waits for them, and re-layouts: 17.6 us -> none  [the longest x2 7.15 us: per_device(): raw_slots = jnp.zeros((capacity, tiles, samples), jnp.bfloat16).at[slot_i...]
    all_to_all x4 -> x0, waiting for transfers between devices: 15.6 us -> none  [the longest x1 13.3 us: per_device(): lax.all_to_all(raw_slots, 'image', split_axis=1, concat_axis=1, tiled=True)]
    another operation x4 -> x0, local copies, waits for them, and re-layouts: 7.79 us -> none  [the longest x2 7.79 us: interpolate(): paired = jnp.stack([stack_tile, shifted], axis=-1)]
    convert_element_type x3 -> x0, other arithmetic: 4.11 us -> none  [the longest x1 3.97 us: per_device(): (gain_part.astype(jnp.float32)[..., None] * filtered).astype(jnp.bfloat16)]
  transfers between devices with their start and end apart: 5 -> 0, of which waited for: 4 -> 0; matrix products, arithmetic and copies ran while one was open for 8% -> 0% of each run, Pallas kernels for 0% -> 0%
where the time goes in v1:
time: 26.9 us; the launch traced here: 26.5 us
  Pallas kernels  22.9 us (85%)
  local copies, waits for them, and re-layouts  3.63 us (13%)
    pallas_call x1, Pallas kernels, per_device(): pl.pallas_call(functools.partial(kernel, split_axis(tiles), groups, half,...  22.9 us
    unnamed x15, local copies, waits for them, and re-layouts  3.63 us

profile of v1, /device:TPU:0, one launch (start us, length us, event | category | flops | bytes accessed | tf_op | source)
XLA Modules:
  0.0 26.5 jit_solution(2460987572876647465)
XLA Ops:
  0.0 0.0 copy-start.4
  0.0 0.0 copy-start.3
  0.0 0.0 copy-start.5
  0.0 0.0 copy-start.6
  0.0 0.7 %copy-done.4 = s32[16,4]{0,1:T(4,128)S(1)} copy-done((s32[16,4]{0,1:T(4,128)S(1)}, s32[16,4]{0,1:T(4,128)}, u32[]{:S(2)}) %copy-start.4) | copy-done | bytes 280
  0.7 0.0 copy-done.3
  0.7 0.0 copy-done.5
  0.7 0.0 copy-done.6
  0.7 0.0 copy-start
  0.7 0.8 %copy-done = bf16[16,1920]{1,0:T(8,128)(2,1)S(1)} copy-done((bf16[16,1920]{1,0:T(8,128)(2,1)S(1)}, bf16[16,1920]{1,0:T(8,128)(2,1)}, u32[]{:S(2)}) %copy-start) | copy-done | bytes 61464
  1.5 0.0 copy-start.1
  1.5 0.8 %copy-done.1 = f32[1,16,512]{2,1,0:T(8,128)S(1)} copy-done((f32[1,16,512]{2,1,0:T(8,128)S(1)}, f32[1,16,512]{2,1,0:T(8,128)}, u32[]{:S(2)}) %copy-start.1) | copy-done | bytes 32792
  2.3 0.0 copy-start.2
  2.3 0.8 %copy-done.2 = f32[1,16,512]{2,1,0:T(8,128)S(1)} copy-done((f32[1,16,512]{2,1,0:T(8,128)S(1)}, f32[1,16,512]{2,1,0:T(8,128)}, u32[]{:S(2)}) %copy-start.2) | copy-done | bytes 32792
  3.1 22.9 %shard_map.73 = f32[1,512]{1,0:T(1,128)S(1)} custom-call(s32[4,16]{1,0:T(4,128)S(1)} %bitcast.8, s32[1,16]{1,0:T(1,128)S(1)} %bitcast.11, s32[4,16]{1,0:T(4,128)S(1)} %bitcast.9, bf16[4,16]{1,0:T(4,128)(2,1)S(1)} %bitcast.10, bf16[16,1920]{1,0:T(8,128)(2,1)S(1)} %copy-done, f32[16,512]{1,0:T(8,128)S(1)} %bitcast.6, f32[16,512]{1,0:T(8,128)S(1)} %bitcast.7), custom_call_target="tpu_custom_call" | custom-call | flops 100000000 | bytes 1000000 | tf_op jit(solution)/shard_map/pallas_call | solution.py:334
  26.0 0.6 %copy.9 = f32[1,512]{1,0:T(1,128)} copy(f32[1,512]{1,0:T(1,128)S(1)} %shard_map.73) | data formatting | bytes 4096
Async XLA Ops:
  0.0 0.7 %copy-start.4 = (s32[16,4]{0,1:T(4,128)S(1)}, s32[16,4]{0,1:T(4,128)}, u32[]{:S(2)}) copy-start(s32[16,4]{0,1:T(4,128)} %param.10) | copy-start | bytes 772
  0.0 0.7 %copy-start.3 = (s32[16,4]{0,1:T(4,128)S(1)}, s32[16,4]{0,1:T(4,128)}, u32[]{:S(2)}) copy-start(s32[16,4]{0,1:T(4,128)} %param.8) | copy-start | bytes 772
  0.0 0.7 %copy-start.5 = (bf16[16,4]{0,1:T(4,128)(2,1)S(1)}, bf16[16,4]{0,1:T(4,128)(2,1)}, u32[]{:S(2)}) copy-start(bf16[16,4]{0,1:T(4,128)(2,1)} %param.11) | copy-start | bytes 388
  0.0 0.7 %copy-start.6 = (s32[16]{0:T(128)S(1)}, s32[16]{0:T(128)}, u32[]{:S(2)}) copy-start(s32[16]{0:T(128)} %param.9) | copy-start | bytes 196
  0.7 0.8 %copy-start = (bf16[16,1920]{1,0:T(8,128)(2,1)S(1)}, bf16[16,1920]{1,0:T(8,128)(2,1)}, u32[]{:S(2)}) copy-start(bf16[16,1920]{1,0:T(8,128)(2,1)} %traces_ref.1) | copy-start | bytes 184324
  1.5 0.8 %copy-start.1 = (f32[1,16,512]{2,1,0:T(8,128)S(1)}, f32[1,16,512]{2,1,0:T(8,128)}, u32[]{:S(2)}) copy-start(f32[1,16,512]{2,1,0:T(8,128)} %param.12) | copy-start | bytes 98308
  2.3 0.8 %copy-start.2 = (f32[1,16,512]{2,1,0:T(8,128)S(1)}, f32[1,16,512]{2,1,0:T(8,128)}, u32[]{:S(2)}) copy-start(f32[1,16,512]{2,1,0:T(8,128)} %param.13) | copy-start | bytes 98308

commit v2 on v1

--- a/solution.py
+++ b/solution.py
@@ -114,10 +114,11 @@
 
 def kernel(
     sizes, groups, half, scale,
-    aperture_ref, bucket_ref, node_ref, gain_ref, traces_ref, travel_ref, spread_ref,
+    aperture_hbm, bucket_hbm, node_hbm, gain_hbm, traces_ref, travel_ref, spread_ref,
     out_ref,
-    blocks, travels, spreads, parts, outgoing,
-    send_sem, recv_sem, table_send, table_recv, part_send, part_recv,
+    aperture_ref, bucket_ref, node_ref, gain_ref,
+    blocks, travels, spreads, parts, outgoing, total_ref,
+    load_sem, send_sem, recv_sem, table_send, table_recv, part_send, part_recv,
 ):
     size_z, size_y, size_c = sizes
     me = lax.axis_index("image")
@@ -132,6 +133,17 @@
     def index(at_z, at_y, at_c):
         return (at_z * size_y + at_y) * size_c + at_c
 
+    loads = [
+        pltpu.make_async_copy(source, landing, load_sem.at[k])
+        for k, (source, landing) in enumerate((
+            (aperture_hbm, aperture_ref), (bucket_hbm, bucket_ref), (node_hbm, node_ref), (gain_hbm, gain_ref),
+            (traces_ref, blocks.at[me, :, pl.ds(0, samples)]),
+            (travel_ref, travels.at[group]), (spread_ref, spreads.at[group]),
+        ))
+    ]
+    for load in loads:
+        load.start()
+
     links_z, links_y, links_c = neighbours(size_z, z), neighbours(size_y, y), neighbours(size_c, core)
     others = [lax.rem(group + r, groups) for r in range(1, groups)]
 
@@ -144,13 +156,17 @@
     for other in others:
         pl.semaphore_signal(barrier, inc=1, device_id=(other, me), device_id_type=MESH)
 
-    blocks[me, :, :samples] = traces_ref[...]
-    blocks[me, :, samples:] = selection(
-        aperture_ref[...], bucket_ref[...], node_ref[...], gain_ref[...], nodes, half
-    ).astype(jnp.bfloat16)
+    with jax.named_scope("selection"):
+        for load in loads[:4]:
+            load.wait()
+        blocks[me, :, samples:] = selection(
+            aperture_ref[...], bucket_ref[...], node_ref[...], gain_ref[...], nodes, half
+        ).astype(jnp.bfloat16)
+        loads[4].wait()
 
     expected = len(others) + sum(1 if cond is None else cond.astype(jnp.int32) for _, cond in partners)
-    pl.semaphore_wait(barrier, expected)
+    with jax.named_scope("entry_barrier"):
+        pl.semaphore_wait(barrier, expected)
 
     started = []
 
@@ -192,6 +208,8 @@
     send_y(me, None)
     send_c(me, None)
     table_copies = []
+    for load in loads[5:]:
+        load.wait()
     for r, other in enumerate(others):
         for which, (source, landing) in enumerate(((travel_ref, travels), (spread_ref, spreads))):
             copy = pltpu.make_async_remote_copy(
@@ -205,6 +223,28 @@
             copy.start()
             table_copies.append(copy)
 
+    plane = size_y * size_c
+    total = plane * count
+
+    def add_plane(at_z, first):
+        mine = pl.ds(at_z * plane, plane)
+        chosen = blocks[mine, :, samples:].reshape(total, 2 * half).astype(jnp.float32)
+        lane = lax.broadcasted_iota(jnp.int32, (1, 2 * half), 1)
+        weight = jnp.sum(jnp.where(lane == me, chosen, 0.0), axis=1, keepdims=True)
+        row = jnp.sum(jnp.where(lane == me + half, chosen, 0.0), axis=1, keepdims=True)
+        rows = lax.broadcasted_iota(jnp.int32, (1, FILTERS * nodes), 1).astype(jnp.float32)
+        member = jnp.where(row == rows, weight, 0.0).astype(jnp.bfloat16)
+        added = lax.dot_general(
+            member,
+            blocks[mine, :, :samples].reshape(total, samples),
+            (((0,), (0,)), ((), ())),
+            preferred_element_type=jnp.float32,
+        )
+        if first:
+            total_ref[...] = added
+        else:
+            total_ref[...] += added
+
     events = []
     along_z = [(0, z, None)]
     for distance, source, valid, step, onward, can in arrivals(size_z, z):
@@ -219,7 +259,8 @@
 
             guarded(valid, run)
 
-        events.append((distance, 0, came_z))
+        events.append((distance, 0, came_z, "from_z_%d" % distance))
+    last_y = size_y - 1
     for far, source_z, valid_z in along_z:
         for distance, source, valid, step, onward, can in arrivals(size_y, y):
 
@@ -235,91 +276,90 @@
 
                 guarded(valid, run)
 
-            events.append((far + distance, 1, came_y))
-    for _, _, run in sorted(events, key=lambda e: e[:2]):
-        run()
-    for _, source, valid, _, _, _ in arrivals(size_c, core):
-        for at_z in range(size_z):
-            for at_y in range(size_y):
-                receive(index(at_z, at_y, source))
-
-    total = size_z * size_y * size_c * count
-    chosen = blocks[:, :, samples:].reshape(total, 2 * half).astype(jnp.float32)
-    lane = lax.broadcasted_iota(jnp.int32, (1, 2 * half), 1)
-    weight = jnp.sum(jnp.where(lane == me, chosen, 0.0), axis=1, keepdims=True)
-    row = jnp.sum(jnp.where(lane == me + half, chosen, 0.0), axis=1, keepdims=True)
-    rows = lax.broadcasted_iota(jnp.int32, (1, FILTERS * nodes), 1).astype(jnp.float32)
-    member = jnp.where(row == rows, weight, 0.0).astype(jnp.bfloat16)
-    stacked = lax.dot_general(
-        member,
-        blocks[:, :, :samples].reshape(total, samples),
-        (((0,), (0,)), ((), ())),
-        preferred_element_type=jnp.float32,
-    )
-    width = samples + LANES
-    stacked = jnp.concatenate([stacked, jnp.zeros((FILTERS * nodes, LANES), jnp.float32)], axis=1)
-    by_bucket = [stacked[b * nodes : (b + 1) * nodes] for b in range(FILTERS)]
-    stack = None
-    for lag in range(MAX_LAG + 1):
-        mixed = None
-        for b in range(FILTERS):
-            if (level := triangle(b, lag)) > 0:
-                term = by_bucket[b] * level
-                mixed = term if mixed is None else mixed + term
-        if lag == 0:
-            stack = mixed
-        else:
-            stack = stack + (pltpu.roll(mixed, lag, 1) + pltpu.roll(mixed, width - lag, 1))
-    upper = pltpu.roll(stack, width - 1, 1)[:, :samples]
-    stack = stack[:, :samples]
-
-    part_copies = []
-    for r, other in enumerate(others):
-        for which, landing in enumerate((travels, spreads)):
+            events.append((far + distance, 1, came_y, "from_y_%d" % far))
+
+        def whole(source_z=source_z, valid_z=valid_z, first=far == 0):
+            def run():
+                for _, source, _, _, _, _ in arrivals(size_c, core):
+                    for at_y in range(size_y):
+                        receive(index(source_z, at_y, source))
+                add_plane(source_z, first)
+
+            guarded(valid_z, run)
+
+        events.append((far + last_y + 1, 2, whole, "plane_%d" % far))
+    for _, _, run, name in sorted(events, key=lambda e: e[:2]):
+        with jax.named_scope(name):
+            run()
+    stacked = total_ref[...]
+    with jax.named_scope("triangle_filter"):
+        width = samples + LANES
+        stacked = jnp.concatenate([stacked, jnp.zeros((FILTERS * nodes, LANES), jnp.float32)], axis=1)
+        by_bucket = [stacked[b * nodes : (b + 1) * nodes] for b in range(FILTERS)]
+        stack = None
+        for lag in range(MAX_LAG + 1):
+            mixed = None
+            for b in range(FILTERS):
+                if (level := triangle(b, lag)) > 0:
+                    term = by_bucket[b] * level
+                    mixed = term if mixed is None else mixed + term
+            if lag == 0:
+                stack = mixed
+            else:
+                stack = stack + (pltpu.roll(mixed, lag, 1) + pltpu.roll(mixed, width - lag, 1))
+        upper = pltpu.roll(stack, width - 1, 1)[:, :samples]
+        stack = stack[:, :samples]
+
+    with jax.named_scope("other_image"):
+        part_copies = []
+        for r, other in enumerate(others):
+            for which, landing in enumerate((travels, spreads)):
+                pltpu.make_async_remote_copy(
+                    src_ref=landing.at[other],
+                    dst_ref=landing.at[other],
+                    send_sem=table_send.at[which, r],
+                    recv_sem=table_recv.at[which, other],
+                    device_id=(other, me),
+                    device_id_type=MESH,
+                ).wait_recv()
+            outgoing[r] = partial_image(stack, upper, travels[other], spreads[other])
+            copy = pltpu.make_async_remote_copy(
+                src_ref=outgoing.at[r],
+                dst_ref=parts.at[group],
+                send_sem=part_send.at[r],
+                recv_sem=part_recv.at[group],
+                device_id=(other, me),
+                device_id_type=MESH,
+            )
+            copy.start()
+            part_copies.append(copy)
+    with jax.named_scope("own_image"):
+        image = partial_image(stack, upper, travels[group], spreads[group])
+    with jax.named_scope("last_waits"):
+        for slot, direction, under, cond in started:
+            copy = pltpu.make_async_remote_copy(
+                src_ref=blocks.at[slot],
+                dst_ref=blocks.at[slot],
+                send_sem=send_sem.at[direction, slot],
+                recv_sem=recv_sem.at[slot],
+                device_id=(group, me),
+                device_id_type=MESH,
+            )
+            guarded(both(under, cond), copy.wait_send)
+        for copy in table_copies:
+            copy.wait_send()
+        for r, other in enumerate(others):
             pltpu.make_async_remote_copy(
-                src_ref=landing.at[other],
-                dst_ref=landing.at[other],
-                send_sem=table_send.at[which, r],
-                recv_sem=table_recv.at[which, other],
+                src_ref=outgoing.at[r],
+                dst_ref=parts.at[other],
+                send_sem=part_send.at[r],
+                recv_sem=part_recv.at[other],
                 device_id=(other, me),
                 device_id_type=MESH,
             ).wait_recv()
-        outgoing[r] = partial_image(stack, upper, travels[other], spreads[other])
-        copy = pltpu.make_async_remote_copy(
-            src_ref=outgoing.at[r],
-            dst_ref=parts.at[group],
-            send_sem=part_send.at[r],
-            recv_sem=part_recv.at[group],
-            device_id=(other, me),
-            device_id_type=MESH,
-        )
-        copy.start()
-        part_copies.append(copy)
-    image = partial_image(stack, upper, travel_ref[...], spread_ref[...])
-    for slot, direction, under, cond in started:
-        copy = pltpu.make_async_remote_copy(
-            src_ref=blocks.at[slot],
-            dst_ref=blocks.at[slot],
-            send_sem=send_sem.at[direction, slot],
-            recv_sem=recv_sem.at[slot],
-            device_id=(group, me),
-            device_id_type=MESH,
-        )
-        guarded(both(under, cond), copy.wait_send)
-    for copy in table_copies:
-        copy.wait_send()
-    for r, other in enumerate(others):
-        pltpu.make_async_remote_copy(
-            src_ref=outgoing.at[r],
-            dst_ref=parts.at[other],
-            send_sem=part_send.at[r],
-            recv_sem=part_recv.at[other],
-            device_id=(other, me),
-            device_id_type=MESH,
-        ).wait_recv()
-        image = image + parts[other]
-    for copy in part_copies:
-        copy.wait_send()
+            image = image + parts[other]
+        for copy in part_copies:
+            copy.wait_send()
     out_ref[...] = image * scale
 
 
@@ -331,17 +371,24 @@
     half = -(-tiles // (LANES // 2)) * (LANES // 2)
     scale = 1.0 / math.sqrt(count * groups * aperture.shape[1])
     vmem = pl.BlockSpec(memory_space=pltpu.VMEM)
+    whole = pl.BlockSpec(memory_space=pl.ANY)
     return pl.pallas_call(
         functools.partial(kernel, split_axis(tiles), groups, half, scale),
         out_shape=jax.ShapeDtypeStruct((1, cells), jnp.float32),
-        in_specs=[vmem] * 7,
+        in_specs=[whole] * 7,
         out_specs=vmem,
         scratch_shapes=[
+            pltpu.VMEM(aperture.shape[::-1], jnp.int32),
+            pltpu.VMEM((1, count), jnp.int32),
+            pltpu.VMEM(table_node.shape[::-1], jnp.int32),
+            pltpu.VMEM(entry_gain.shape[::-1], jnp.bfloat16),
             pltpu.VMEM((tiles, count, samples + 2 * half), jnp.bfloat16),
             pltpu.VMEM((groups, nodes, cells), jnp.float32),
             pltpu.VMEM((groups, nodes, cells), jnp.float32),
             pltpu.VMEM((groups, 1, cells), jnp.float32),
             pltpu.VMEM((max(groups - 1, 1), 1, cells), jnp.float32),
+            pltpu.VMEM((FILTERS * nodes, samples), jnp.float32),
+            pltpu.SemaphoreType.DMA((7,)),
             pltpu.SemaphoreType.DMA((6, tiles)),
             pltpu.SemaphoreType.DMA((tiles,)),
             pltpu.SemaphoreType.DMA((2, max(groups - 1, 1))),
@@ -350,7 +397,7 @@
             pltpu.SemaphoreType.DMA((groups,)),
         ],
         compiler_params=pltpu.CompilerParams(
-            collective_id=0, has_side_effects=True, vmem_limit_bytes=48 * 1024 * 1024
+            collective_id=0, has_side_effects=True, vmem_limit_bytes=56 * 1024 * 1024
         ),
         cost_estimate=pl.CostEstimate(flops=10**8, bytes_accessed=10**6, transcendentals=0),
     )(aperture.T, bucket.reshape(1, count), table_node.T, entry_gain.T, traces, travel[0], spread[0])

time: 26.9 us -> 25.6 us (0.952)
  local copies, waits for them, and re-layouts: 3.63 us -> 1.26 us
  Pallas kernels: 22.9 us -> 24.2 us
    unnamed x15 -> x1, local copies, waits for them, and re-layouts: 3.63 us -> 1.26 us
    pallas_call x1, Pallas kernels: 22.9 us -> 24.2 us  [per_device(): pl.pallas_call(functools.partial(kernel, split_axis(tiles), groups, half,...]
where the time goes in v2:
time: 25.6 us; the launch traced here: 25.5 us
  Pallas kernels  24.2 us (95%)
  local copies, waits for them, and re-layouts  1.26 us (5%)
    pallas_call x1, Pallas kernels, per_device(): pl.pallas_call(functools.partial(kernel, split_axis(tiles), groups, half,...  24.2 us
    unnamed x1, local copies, waits for them, and re-layouts  1.26 us

profile of v2, /device:TPU:0, one launch (start us, length us, event | category | flops | bytes accessed | tf_op | source)
XLA Modules:
  0.0 25.5 jit_solution(13673468162796756633)
XLA Ops:
  0.0 24.2 %shard_map.73 = f32[1,512]{1,0:T(1,128)} custom-call(s32[4,16]{1,0:T(4,128)} %bitcast.8, s32[1,16]{1,0:T(1,128)} %bitcast.11, s32[4,16]{1,0:T(4,128)} %bitcast.9, bf16[4,16]{1,0:T(4,128)(2,1)} %bitcast.10, bf16[16,1920]{1,0:T(8,128)(2,1)} %traces_ref.1, f32[16,512]{1,0:T(8,128)} %bitcast.6, f32[16,512]{1,0:T(8,128)} %bitcast.7), custom_call_target="tpu_custom_call" | custom-call | flops 100000000 | bytes 1000000 | tf_op jit(solution)/shard_map/pallas_call | solution.py:375
  24.2 1.3 %copy.9 = f32[1,512]{1,0:T(1,128)} copy(f32[1,512]{1,0:T(1,128)} %shard_map.73) | data formatting | bytes 4096

commit v3 on v2

--- a/solution.py
+++ b/solution.py
@@ -23,41 +23,18 @@
     return (count, 1, 1)
 
 
-def both(first, second):
-    if first is None:
-        return second
-    if second is None:
-        return first
-    return jnp.logical_and(first, second)
-
-
-def guarded(cond, action):
-    if cond is None:
-        action()
-    else:
-        pl.when(cond)(action)
-
-
-def neighbours(size, at):
-    if size == 1:
-        return []
-    if size == 2:
-        return [(1, 1 - at, None)]
-    return [(1, at + 1, at < size - 1), (-1, at - 1, at > 0)]
-
-
-def arrivals(size, at):
-    if size == 1:
-        return []
-    if size == 2:
-        return [(1, 1 - at, None, 1, None, None)]
+def peers(size, at):
     found = []
-    for distance in range(1, size):
-        for step in (1, -1):
-            source = at - step * distance
-            valid = source >= 0 if step > 0 else source < size
-            onward = at < size - 1 if step > 0 else at > 0
-            found.append((distance, source, valid, step, at + step, onward))
+    for step in range(1, size):
+        if size & (size - 1):
+            found.append(lax.rem(at + step, size))
+            continue
+        to, bit = at, 1
+        while bit <= step:
+            if step & bit:
+                to = to + bit * (1 - 2 * lax.rem(to // bit, 2))
+            bit *= 2
+        found.append(to)
     return found
 
 
@@ -144,17 +121,16 @@
     for load in loads:
         load.start()
 
-    links_z, links_y, links_c = neighbours(size_z, z), neighbours(size_y, y), neighbours(size_c, core)
+    line_z, line_y, line_c = peers(size_z, z), peers(size_y, y), peers(size_c, core)
     others = [lax.rem(group + r, groups) for r in range(1, groups)]
 
     barrier = pltpu.get_barrier_semaphore()
-    partners = [(index(to, y, core), cond) for _, to, cond in links_z]
-    partners += [(index(z, to, core), cond) for _, to, cond in links_y]
-    partners += [(index(z, y, to), cond) for _, to, cond in links_c]
-    for to, cond in partners:
-        guarded(cond, lambda to=to: pl.semaphore_signal(barrier, inc=1, device_id=(group, to), device_id_type=MESH))
-    for other in others:
-        pl.semaphore_signal(barrier, inc=1, device_id=(other, me), device_id_type=MESH)
+    partners = [(group, index(to, y, core)) for to in line_z]
+    partners += [(group, index(z, to, core)) for to in line_y]
+    partners += [(group, index(z, y, to)) for to in line_c]
+    partners += [(other, me) for other in others]
+    for partner in partners:
+        pl.semaphore_signal(barrier, inc=1, device_id=partner, device_id_type=MESH)
 
     with jax.named_scope("selection"):
         for load in loads[:4]:
@@ -164,49 +140,43 @@
         ).astype(jnp.bfloat16)
         loads[4].wait()
 
-    expected = len(others) + sum(1 if cond is None else cond.astype(jnp.int32) for _, cond in partners)
     with jax.named_scope("entry_barrier"):
-        pl.semaphore_wait(barrier, expected)
+        pl.semaphore_wait(barrier, len(partners))
 
     started = []
 
-    def send(slot, direction, to, cond, under=None):
-        copy = pltpu.make_async_remote_copy(
+    def block_copy(slot, lane, to):
+        return pltpu.make_async_remote_copy(
             src_ref=blocks.at[slot],
             dst_ref=blocks.at[slot],
-            send_sem=send_sem.at[direction, slot],
+            send_sem=send_sem.at[lane, slot],
             recv_sem=recv_sem.at[slot],
             device_id=(group, to),
             device_id_type=MESH,
         )
-        guarded(cond, copy.start)
-        started.append((slot, direction, under, cond))
-
-    def receive(slot):
-        pltpu.make_async_remote_copy(
-            src_ref=blocks.at[slot],
-            dst_ref=blocks.at[slot],
-            send_sem=send_sem.at[0, slot],
-            recv_sem=recv_sem.at[slot],
-            device_id=(group, me),
-            device_id_type=MESH,
-        ).wait_recv()
-
-    def number(base, step):
-        return base if step > 0 else base + 1
-
-    def send_y(slot, under):
-        for step, to, cond in links_y:
-            send(slot, number(2, step), index(z, to, core), cond, under)
-
-    def send_c(slot, under):
-        for step, to, cond in links_c:
-            send(slot, number(4, step), index(z, y, to), cond, under)
-
-    for step, to, cond in links_z:
-        send(me, number(0, step), index(to, y, core), cond)
-    send_y(me, None)
-    send_c(me, None)
+
+    def send(slot, lane, to):
+        copy = block_copy(slot, lane, to)
+        copy.start()
+        started.append(copy)
+
+    def receive(slot, source):
+        block_copy(slot, 0, source).wait_recv()
+
+    first_y, first_c = size_z - 1, size_z + size_y - 2
+
+    def send_y(slot):
+        for k, to in enumerate(line_y):
+            send(slot, first_y + k, index(z, to, core))
+
+    def send_c(slot):
+        for k, to in enumerate(line_c):
+            send(slot, first_c + k, index(z, y, to))
+
+    for k, to in enumerate(line_z):
+        send(me, k, index(to, y, core))
+    send_y(me)
+    send_c(me)
     table_copies = []
     for load in loads[5:]:
         load.wait()
@@ -245,52 +215,33 @@
         else:
             total_ref[...] += added
 
-    events = []
-    along_z = [(0, z, None)]
-    for distance, source, valid, step, onward, can in arrivals(size_z, z):
-        along_z.append((distance, source, valid))
-
-        def came_z(slot=index(source, y, core), valid=valid, step=step, onward=onward, can=can):
-            def run():
-                receive(slot)
-                send(slot, number(0, step), index(onward, y, core), can, valid)
-                send_y(slot, valid)
-                send_c(slot, valid)
-
-            guarded(valid, run)
-
-        events.append((distance, 0, came_z, "from_z_%d" % distance))
-    last_y = size_y - 1
-    for far, source_z, valid_z in along_z:
-        for distance, source, valid, step, onward, can in arrivals(size_y, y):
-
-            def came_y(
-                slot=index(source_z, source, core),
-                valid=both(valid_z, valid), step=step, onward=onward, can=can,
-            ):
-                def run():
-                    receive(slot)
-                    if onward is not None:
-                        send(slot, number(2, step), index(z, onward, core), can, valid)
-                    send_c(slot, valid)
-
-                guarded(valid, run)
-
-            events.append((far + distance, 1, came_y, "from_y_%d" % far))
-
-        def whole(source_z=source_z, valid_z=valid_z, first=far == 0):
-            def run():
-                for _, source, _, _, _, _ in arrivals(size_c, core):
-                    for at_y in range(size_y):
-                        receive(index(source_z, at_y, source))
-                add_plane(source_z, first)
-
-            guarded(valid_z, run)
-
-        events.append((far + last_y + 1, 2, whole, "plane_%d" % far))
-    for _, _, run, name in sorted(events, key=lambda e: e[:2]):
-        with jax.named_scope(name):
-            run()
+    def from_z(at_z):
+        slot = index(at_z, y, core)
+        receive(slot, slot)
+        send_y(slot)
+        send_c(slot)
+
+    def from_y(at_z):
+        for at_y in line_y:
+            slot = index(at_z, at_y, core)
+            receive(slot, slot)
+            send_c(slot)
+
+    def from_c(at_z, first):
+        for at_c in line_c:
+            for at_y in [y, *line_y]:
+                slot = index(at_z, at_y, at_c)
+                receive(slot, index(z, y, at_c))
+        add_plane(at_z, first)
+
+    planes = [z, *line_z]
+    for k in range(size_z + 2):
+        if 1 <= k < size_z:
+            from_z(planes[k])
+        if 1 <= k <= size_z:
+            from_y(planes[k - 1])
+        if k >= 2:
+            from_c(planes[k - 2], k == 2)
     stacked = total_ref[...]
     with jax.named_scope("triangle_filter"):
         width = samples + LANES
@@ -336,16 +287,8 @@
     with jax.named_scope("own_image"):
         image = partial_image(stack, upper, travels[group], spreads[group])
     with jax.named_scope("last_waits"):
-        for slot, direction, under, cond in started:
-            copy = pltpu.make_async_remote_copy(
-                src_ref=blocks.at[slot],
-                dst_ref=blocks.at[slot],
-                send_sem=send_sem.at[direction, slot],
-                recv_sem=recv_sem.at[slot],
-                device_id=(group, me),
-                device_id_type=MESH,
-            )
-            guarded(both(under, cond), copy.wait_send)
+        for copy in started:
+            copy.wait_send()
         for copy in table_copies:
             copy.wait_send()
         for r, other in enumerate(others):
@@ -369,11 +312,12 @@
     count, samples = traces.shape
     nodes, cells = travel.shape[1], travel.shape[2]
     half = -(-tiles // (LANES // 2)) * (LANES // 2)
+    sizes = split_axis(tiles)
     scale = 1.0 / math.sqrt(count * groups * aperture.shape[1])
     vmem = pl.BlockSpec(memory_space=pltpu.VMEM)
     whole = pl.BlockSpec(memory_space=pl.ANY)
     return pl.pallas_call(
-        functools.partial(kernel, split_axis(tiles), groups, half, scale),
+        functools.partial(kernel, sizes, groups, half, scale),
         out_shape=jax.ShapeDtypeStruct((1, cells), jnp.float32),
         in_specs=[whole] * 7,
         out_specs=vmem,
@@ -389,7 +333,7 @@
             pltpu.VMEM((max(groups - 1, 1), 1, cells), jnp.float32),
             pltpu.VMEM((FILTERS * nodes, samples), jnp.float32),
             pltpu.SemaphoreType.DMA((7,)),
-            pltpu.SemaphoreType.DMA((6, tiles)),
+            pltpu.SemaphoreType.DMA((max(sum(sizes) - 3, 1), tiles)),
             pltpu.SemaphoreType.DMA((tiles,)),
             pltpu.SemaphoreType.DMA((2, max(groups - 1, 1))),
             pltpu.SemaphoreType.DMA((2, groups)),

time: 25.6 us -> 23.4 us (0.914)
  Pallas kernels: 24.2 us -> 22 us
    pallas_call x1, Pallas kernels: 24.2 us -> 22 us  [per_device(): pl.pallas_call(functools.partial(kernel, sizes, groups, half, scale), out...]
where the time goes in v3:
time: 23.4 us; the launch traced here: 23.2 us
  Pallas kernels  22 us (94%)
  local copies, waits for them, and re-layouts  1.26 us (5%)
    pallas_call x1, Pallas kernels, per_device(): pl.pallas_call(functools.partial(kernel, sizes, groups, half, scale), out...  22 us
    unnamed x1, local copies, waits for them, and re-layouts  1.26 us

profile of v3, /device:TPU:0, one launch (start us, length us, event | category | flops | bytes accessed | tf_op | source)
XLA Modules:
  0.0 23.2 jit_solution(16650596493503242999)
XLA Ops:
  0.0 22.0 %shard_map.73 = f32[1,512]{1,0:T(1,128)} custom-call(s32[4,16]{1,0:T(4,128)} %bitcast.8, s32[1,16]{1,0:T(1,128)} %bitcast.11, s32[4,16]{1,0:T(4,128)} %bitcast.9, bf16[4,16]{1,0:T(4,128)(2,1)} %bitcast.10, bf16[16,1920]{1,0:T(8,128)(2,1)} %traces_ref.1, f32[16,512]{1,0:T(8,128)} %bitcast.6, f32[16,512]{1,0:T(8,128)} %bitcast.7), custom_call_target="tpu_custom_call" | custom-call | flops 100000000 | bytes 1000000 | tf_op jit(solution)/shard_map/pallas_call | solution.py:319
  22.0 1.3 %copy.9 = f32[1,512]{1,0:T(1,128)} copy(f32[1,512]{1,0:T(1,128)} %shard_map.73) | data formatting | bytes 4096

commit v4 on v3

--- a/solution.py
+++ b/solution.py
@@ -110,21 +110,27 @@
     def index(at_z, at_y, at_c):
         return (at_z * size_y + at_y) * size_c + at_c
 
+    home = (z * size_c + core) * size_y + y
     loads = [
         pltpu.make_async_copy(source, landing, load_sem.at[k])
         for k, (source, landing) in enumerate((
             (aperture_hbm, aperture_ref), (bucket_hbm, bucket_ref), (node_hbm, node_ref), (gain_hbm, gain_ref),
-            (traces_ref, blocks.at[me, :, pl.ds(0, samples)]),
+            (traces_ref, blocks.at[home, :, pl.ds(0, samples)]),
             (travel_ref, travels.at[group]), (spread_ref, spreads.at[group]),
         ))
     ]
     for load in loads:
         load.start()
 
+    def place(at_z, at_y, at_c):
+        return (at_z * size_c + at_c) * size_y + at_y
+
     line_z, line_y, line_c = peers(size_z, z), peers(size_y, y), peers(size_c, core)
     others = [lax.rem(group + r, groups) for r in range(1, groups)]
 
     barrier = pltpu.get_barrier_semaphore()
+    if size_z == 4:
+        line_z = [line_z[0], line_z[2], line_z[1]]
     partners = [(group, index(to, y, core)) for to in line_z]
     partners += [(group, index(z, to, core)) for to in line_y]
     partners += [(group, index(z, y, to)) for to in line_c]
@@ -135,7 +141,7 @@
     with jax.named_scope("selection"):
         for load in loads[:4]:
             load.wait()
-        blocks[me, :, samples:] = selection(
+        blocks[home, :, samples:] = selection(
             aperture_ref[...], bucket_ref[...], node_ref[...], gain_ref[...], nodes, half
         ).astype(jnp.bfloat16)
         loads[4].wait()
@@ -163,23 +169,27 @@
     def receive(slot, source):
         block_copy(slot, 0, source).wait_recv()
 
+    def line_copy(at_z, at_c, lane, to):
+        first = place(at_z, 0, at_c)
+        return pltpu.make_async_remote_copy(
+            src_ref=blocks.at[pl.ds(first, size_y)],
+            dst_ref=blocks.at[pl.ds(first, size_y)],
+            send_sem=send_sem.at[lane, first],
+            recv_sem=recv_sem.at[first],
+            device_id=(group, to),
+            device_id_type=MESH,
+        )
+
     first_y, first_c = size_z - 1, size_z + size_y - 2
 
     def send_y(slot):
         for k, to in enumerate(line_y):
             send(slot, first_y + k, index(z, to, core))
 
-    def send_c(slot):
-        for k, to in enumerate(line_c):
-            send(slot, first_c + k, index(z, y, to))
-
+    send_y(home)
     for k, to in enumerate(line_z):
-        send(me, k, index(to, y, core))
-    send_y(me)
-    send_c(me)
+        send(home, k, index(to, y, core))
     table_copies = []
-    for load in loads[5:]:
-        load.wait()
     for r, other in enumerate(others):
         for which, (source, landing) in enumerate(((travel_ref, travels), (spread_ref, spreads))):
             copy = pltpu.make_async_remote_copy(
@@ -216,22 +226,21 @@
             total_ref[...] += added
 
     def from_z(at_z):
-        slot = index(at_z, y, core)
-        receive(slot, slot)
+        slot = place(at_z, y, core)
+        receive(slot, index(at_z, y, core))
         send_y(slot)
-        send_c(slot)
 
     def from_y(at_z):
         for at_y in line_y:
-            slot = index(at_z, at_y, core)
-            receive(slot, slot)
-            send_c(slot)
+            receive(place(at_z, at_y, core), index(z, at_y, core))
+        for k, to in enumerate(line_c):
+            copy = line_copy(at_z, core, first_c + k, index(z, y, to))
+            copy.start()
+            started.append(copy)
 
     def from_c(at_z, first):
         for at_c in line_c:
-            for at_y in [y, *line_y]:
-                slot = index(at_z, at_y, at_c)
-                receive(slot, index(z, y, at_c))
+            line_copy(at_z, at_c, 0, index(z, y, at_c)).wait_recv()
         add_plane(at_z, first)
 
     planes = [z, *line_z]
@@ -285,6 +294,8 @@
             copy.start()
             part_copies.append(copy)
     with jax.named_scope("own_image"):
+        for load in loads[5:]:
+            load.wait()
         image = partial_image(stack, upper, travels[group], spreads[group])
     with jax.named_scope("last_waits"):
         for copy in started:

time: 23.4 us -> 23.4 us (level)
  no operation moved by 1% of the time
where the time goes in v4:
time: 23.4 us; the launch traced here: 23.2 us
  Pallas kernels  21.9 us (94%)
  local copies, waits for them, and re-layouts  1.26 us (5%)
    pallas_call x1, Pallas kernels, per_device(): pl.pallas_call(functools.partial(kernel, sizes, groups, half, scale), out...  21.9 us
    unnamed x1, local copies, waits for them, and re-layouts  1.26 us

profile of v4, /device:TPU:0, one launch (start us, length us, event | category | flops | bytes accessed | tf_op | source)
XLA Modules:
  0.0 23.2 jit_solution(13437901369900102544)
XLA Ops:
  0.0 21.9 %shard_map.73 = f32[1,512]{1,0:T(1,128)} custom-call(s32[4,16]{1,0:T(4,128)} %bitcast.8, s32[1,16]{1,0:T(1,128)} %bitcast.11, s32[4,16]{1,0:T(4,128)} %bitcast.9, bf16[4,16]{1,0:T(4,128)(2,1)} %bitcast.10, bf16[16,1920]{1,0:T(8,128)(2,1)} %traces_ref.1, f32[16,512]{1,0:T(8,128)} %bitcast.6, f32[16,512]{1,0:T(8,128)} %bitcast.7), custom_call_target="tpu_custom_call" | custom-call | flops 100000000 | bytes 1000000 | tf_op jit(solution)/shard_map/pallas_call | solution.py:330
  21.9 1.3 %copy.9 = f32[1,512]{1,0:T(1,128)} copy(f32[1,512]{1,0:T(1,128)} %shard_map.73) | data formatting | bytes 4096
